TPU v7x, 32 devices: a whole 2x2x4 slice. The times are simulated.
32 devices in a mesh: replica: 16 (over z, y, x), tensor: 2 (over core).
Axes of the slice: x: 2, y: 2, z: 4, core: 2. Of those that a mesh axis runs over, the one named last changes fastest.
Arguments:
- features: bfloat16 [1024, 4, 7680], P('replica', None, 'tensor'), may hold values from -6 to 6
- kv_weight: bfloat16 [7680, 8, 256], P('tensor'), may hold values from -0.0625 to 0.0625
- image_owner: int32 [1024], replicated, may hold values from 0 to 15, as said below
- image_request: int32 [1024], replicated, may hold values from 0 to 7, as said below
- cross_query: bfloat16 [128, 64, 128], P('replica', 'tensor'), may hold values from -6 to 6
- self_query: bfloat16 [128, 64, 128], P('replica', 'tensor'), may hold values from -2.5 to 2.5
- self_cache: bfloat16 [128, 128, 8, 256], P('replica', None, 'tensor'), may hold values from -2.5 to 2.5
- fresh_key_value: bfloat16 [128, 8, 256], P('replica', 'tensor'), may hold values from -2.5 to 2.5
- cache_len: int32 [128], P('replica'), may hold values from 1 to 128, 8192 in all
Outputs:
- cross_out: bfloat16 [128, 64, 128], P('replica', 'tensor')
- self_out: bfloat16 [128, 64, 128], P('replica', 'tensor')
Inputs may be any that keep to these rules, and one draw needn't show every extreme that they name: `image_owner`: within each aligned block of 64 consecutive images (the images of one replica group), no decode replica owns more than 8 images, and one decode replica owns exactly 8 images in every block. `image_request`: some requests have no image.
All inputs are finite; a program needn't handle non-finite values. No bound on the sum of `cache_len` on one device may be relied on, other than what follows from the above.
Results may differ from a plain program's by a relative error of at most 0.02.
Values may be sent and summed in bfloat16 or wider, within the bound.
A program may use at most 128 MiB of HBM per device.

v0:
```python
import math

import jax
import jax.numpy as jnp
from jax import lax
from jax.sharding import PartitionSpec as P


def local(
    features,
    kv_weight,
    image_owner,
    image_request,
    cross_query,
    self_query,
    self_cache,
    fresh_key_value,
    cache_len,
):
    n_rep = lax.axis_size("replica")
    me_rep = lax.axis_index("replica")
    images, patches, block = features.shape
    kvh_all = kv_weight.shape[1]
    width2 = kv_weight.shape[2]
    head_width = width2 // 2
    score_scale = 1.0 / math.sqrt(head_width)
    slot_cap = max(2, 2 * images // n_rep)
    slot_all = n_rep * slot_cap
    owners = image_owner.reshape(n_rep, images)
    requests = image_request.reshape(n_rep, images)
    own_block = lax.dynamic_index_in_dim(owners, me_rep, 0, keepdims=False)
    positions = jnp.arange(images, dtype=jnp.int32)
    same_owner = own_block[:, None] == own_block[None, :]
    earlier = positions[:, None] > positions[None, :]
    rank = jnp.sum((same_owner & earlier).astype(jnp.int32), axis=1, dtype=jnp.int32)
    slot = own_block * slot_cap + rank
    placing = (jnp.arange(slot_all, dtype=jnp.int32)[:, None] == slot[None, :]).astype(jnp.bfloat16)
    weight_flat = kv_weight.reshape(block, kvh_all * width2)
    sq_heads = self_query.shape[1]
    kvh_local = self_cache.shape[2]
    group = sq_heads // kvh_local
    req_count = self_query.shape[0]
    self_query_rows = self_query.reshape(req_count, kvh_local, group, head_width)
    scores = (
        jnp.einsum(
            "bkgd,bskd->bkgs",
            self_query_rows,
            self_cache[..., :head_width],
            preferred_element_type=jnp.float32,
        )
        * score_scale
    )
    live = jnp.arange(self_cache.shape[1], dtype=jnp.int32)[None, :] < cache_len[:, None]
    weight = jnp.where(live[:, None, None, :], jnp.exp(scores), jnp.float32(0.0))
    fresh_weight = jnp.exp(
        jnp.einsum(
            "ptwe,pte->ptw",
            self_query_rows,
            fresh_key_value[..., :head_width],
            preferred_element_type=jnp.float32,
        )
        * score_scale
    )
    total = jnp.sum(weight, axis=-1) + fresh_weight
    numer = jnp.einsum(
        "bkgs,bskd->bkgd",
        weight.astype(jnp.bfloat16),
        self_cache[..., head_width:],
        preferred_element_type=jnp.float32,
    )
    numer = numer + fresh_weight.astype(jnp.bfloat16).astype(jnp.float32)[
        ..., None
    ] * fresh_key_value[:, :, None, head_width:].astype(jnp.float32)
    self_out = (
        (numer / total[..., None]).astype(jnp.bfloat16).reshape(req_count, sq_heads, head_width)
    )
    outgoing = jnp.dot(
        placing, features.reshape(images, patches * block), preferred_element_type=jnp.float32
    )
    outgoing = outgoing.astype(jnp.bfloat16).reshape(n_rep, slot_cap, patches * block)
    arrived = lax.all_to_all(outgoing, "replica", split_axis=0, concat_axis=0, tiled=True)
    count = arrived.shape[1]
    flat = arrived.reshape(n_rep * count * patches, block)
    product = jnp.dot(flat, weight_flat, preferred_element_type=jnp.float32)
    partial_value = product.reshape(n_rep, count, patches, kvh_all, width2)
    summed = lax.psum_scatter(
        partial_value.astype(jnp.bfloat16), "tensor", scatter_dimension=3, tiled=True
    )
    image_kv = summed.reshape(slot_all * patches, kvh_local, width2)
    owner_match = (owners == me_rep).astype(jnp.int32)
    rank_all = jnp.cumsum(owner_match, axis=1, dtype=jnp.int32) - owner_match
    slot_ids = jnp.arange(slot_cap, dtype=jnp.int32)
    chosen = owner_match[:, None, :] * (rank_all[:, None, :] == slot_ids[None, :, None]).astype(
        jnp.int32
    )
    slot_live = jnp.sum(chosen, axis=-1, dtype=jnp.int32)
    slot_req = jnp.sum(chosen * requests[:, None, :], axis=-1, dtype=jnp.int32)
    row_live = (
        jnp.broadcast_to(slot_live[:, :, None], (n_rep, slot_cap, patches)).reshape(
            slot_all * patches
        )
        > 0
    )
    row_req = jnp.broadcast_to(slot_req[:, :, None], (n_rep, slot_cap, patches)).reshape(
        slot_all * patches
    )
    unscaled_keys = image_kv[..., :head_width].astype(jnp.float32)
    image_keys = (
        unscaled_keys
        * lax.rsqrt(jnp.mean(unscaled_keys * unscaled_keys, axis=-1, keepdims=True) + 1e-05)
    ).astype(jnp.bfloat16)
    image_values = image_kv[..., head_width:]
    cquery = cross_query.reshape(req_count, kvh_local, group, head_width)
    cscores = (
        jnp.einsum("bkgd,skd->bkgs", cquery, image_keys, preferred_element_type=jnp.float32)
        * score_scale
    )
    mask = row_live[None, :] & (row_req[None, :] == jnp.arange(req_count, dtype=jnp.int32)[:, None])
    cweight = jnp.where(mask[:, None, None, :], jnp.exp(cscores), jnp.float32(0.0))
    ctotal = jnp.sum(cweight, axis=-1)
    cnumer = jnp.einsum(
        "bkgs,skd->bkgd",
        cweight.astype(jnp.bfloat16),
        image_values,
        preferred_element_type=jnp.float32,
    )
    has_image = jnp.any(mask, axis=1)
    safe = jnp.where(has_image[:, None, None], ctotal, jnp.float32(1.0))
    cross_out = jnp.where(
        has_image[:, None, None, None], cnumer / safe[..., None], jnp.float32(0.0)
    )
    cross_out = cross_out.astype(jnp.bfloat16).reshape(req_count, sq_heads, head_width)
    return (cross_out, self_out)


def solution(mesh):
    return jax.shard_map(
        local,
        mesh=mesh,
        in_specs=(
            P("replica", None, "tensor"),
            P("tensor", None, None),
            P(),
            P(),
            P("replica", "tensor", None),
            P("replica", "tensor", None),
            P("replica", None, "tensor", None),
            P("replica", "tensor", None),
            P("replica"),
        ),
        out_specs=(P("replica", "tensor", None), P("replica", "tensor", None)),
        check_vma=False,
    )
```

profile of v0, /device:TPU:8, one launch (start us, length us, event | category | flops | bytes accessed | tf_op | source)
XLA Modules:
  0.0 155.2 jit_solution(8019762902789372809)
XLA Ops:
  7.2 0.0 copy-start
  7.2 0.8 reshape.137
  8.0 0.2 convert_reduce_fusion
  8.2 1.7 %copy.95 = bf16[8,8,4,3840]{3,1,2,0:T(8,128)(2,1)S(1)} copy(bf16[8,8,4,3840]{3,2,1,0:T(4,128)(2,1)} %bitcast.93) | data formatting | bytes 3932160
  9.9 3.1 %fusion = bf16[16,8,15360]{2,1,0:T(8,128)(2,1)} fusion(bf16[64,15360]{1,0:T(8,128)(2,1)S(1)} %bitcast.89, s32[64]{0:T(128)S(1)} %fusion.32), kind=kOutput, calls=%fused_computation.1 | convolution fusion | flops 253632512 | bytes 5898496 | tf_op jit(solution)/shard_map/dot_general | solution.py:77
  13.0 7.2 %all-to-all-start = ((bf16[16,8,15360]{2,1,0:T(8,128)(2,1)}), bf16[16,8,15360]{2,1,0:T(8,128)(2,1)}, u32[]{:S(2)}, u32[]{:S(2)}) async-start(bf16[16,8,15360]{2,1,0:T(8,128)(2,1)} %fusion), calls=%async_computation | async-start | bytes 7864320 | tf_op jit(solution)/shard_map/all_to_all | solution.py:81
  20.2 0.0 all-reduce.3.cloned.1.call-start
  20.3 15.2 %copy.96 = bf16[480,8,8,256]{3,1,2,0:T(8,128)(2,1)} copy(bf16[480,8,8,256]{3,2,1,0:T(8,128)(2,1)} %bitcast.87) | data formatting | bytes 31457280
  35.5 0.0 copy-start.3
  35.5 19.4 %copy.64 = bf16[2048,3840]{1,0:T(8,128)(2,1)} copy(bf16[2048,3840]{0,1:T(8,128)(2,1)} %bitcast.86) | data formatting | bytes 31457280 | tf_op jit(solution)/shard_map/dot_general | solution.py:84
  54.9 0.2 reduce_window_sum.11
  55.1 0.0 copy-done.3
  55.1 0.1 mul.70
  55.2 50.3 %all-to-all-done = bf16[16,8,15360]{2,1,0:T(8,128)(2,1)} async-done(((bf16[16,8,15360]{2,1,0:T(8,128)(2,1)}), bf16[16,8,15360]{2,1,0:T(8,128)(2,1)}, u32[]{:S(2)}, u32[]{:S(2)}) %all-to-all-start) | async-done | bytes 3932192 | tf_op jit(solution)/shard_map/all_to_all | solution.py:81
  105.4 0.0 copy-start.5
  105.4 0.0 copy-start.2
  105.4 0.0 copy-start.4
  105.5 13.9 %convolution_convert_fusion.1 = bf16[16,8,4,8,256]{4,1,3,2,0:T(8,128)(2,1)} fusion(bf16[16,8,4,3840,1]{3,1,4,2,0:T(8,128)(2,1)} %bitcast.6, bf16[8,256,3840,1,1]{2,1,0,4,3:T(8,128)(2,1)} %bitcast.88), kind=kOutput, calls=%fused_computation.2 | convolution fusion | flops 8054112256 | bytes 21757952 | tf_op jit(solution)/shard_map/dot_general | solution.py:84
  119.4 0.0 copy-start.1
  119.4 0.0 all-reduce.3.cloned.1.call-update
  119.4 0.6 select_reduce_fusion
  120.0 0.1 broadcast_in_dim.43
  120.1 0.1 eq.84
  120.2 0.1 broadcast_in_dim.38
  120.3 0.1 gt.29
  120.4 0.0 copy-done.5
  120.5 0.1 iota_compare_fusion.5
  120.5 0.0 copy-done.2
  120.5 0.0 copy-done.4
  120.6 0.1 fusion.26
  120.7 0.3 copy-done.1
  121.0 0.7 fusion.36
  121.7 0.7 fusion.37
  122.5 0.0 copy-done.6
  122.5 0.6 dynamic-slice
  123.7 1.0 fusion.11
  124.8 0.1 fusion.35
  124.9 18.7 %all-reduce.3.cloned.1.call-done = bf16[16,8,4,8,256]{4,1,3,2,0:T(8,128)(2,1)} async-done(((bf16[16,8,4,8,256]{4,1,3,2,0:T(8,128)(2,1)}), bf16[16,8,4,8,256]{4,1,3,2,0:T(8,128)(2,1)}) %all-reduce.3.cloned.1.call-update) | async-done | bytes 2097168
  143.6 1.3 constant_dynamic-slice_fusion
  144.9 0.5 copy.65
  145.4 0.6 fusion.12
  146.1 0.2 slice.24
  146.3 0.7 fusion.16
  147.0 0.0 copy-done
  147.0 0.4 fusion.38
  147.4 0.1 broadcast_select_fusion
  147.5 0.2 fusion.10
  147.8 0.6 copy.130
  (11 shorter events, 0.1 us)
Async XLA Ops:
  7.2 139.9 %copy-start = (bf16[8,32,128]{2,1,0:T(8,128)(2,1)S(1)}, bf16[8,32,128]{2,1,0:T(8,128)(2,1)}, u32[]{:S(2)}) copy-start(bf16[8,32,128]{2,1,0:T(8,128)(2,1)} %param.13) | copy-start | bytes 196612
  13.0 92.5 %all-to-all-start = ((bf16[16,8,15360]{2,1,0:T(8,128)(2,1)}), bf16[16,8,15360]{2,1,0:T(8,128)(2,1)}, u32[]{:S(2)}, u32[]{:S(2)}) async-start(bf16[16,8,15360]{2,1,0:T(8,128)(2,1)} %fusion), calls=%async_computation | async-start | bytes 7864320 | tf_op jit(solution)/shard_map/all_to_all | solution.py:81
  20.2 123.4 %all-reduce.3.cloned.1.call-start = ((), (), s32[]{:S(2)}) async-start(), calls=%async_computation.1 | async-start | bytes 4194304
  35.5 19.6 %copy-start.3 = (s32[1024]{0:T(1024)S(1)}, s32[1024]{0:T(1024)}, u32[]{:S(2)}) copy-start(s32[1024]{0:T(1024)} %param.12) | copy-start | bytes 12292
  105.4 15.0 %copy-start.5 = (s32[8]{0:T(128)S(1)}, s32[8]{0:T(128)}, u32[]{:S(2)}) copy-start(s32[8]{0:T(128)} %param.17) | copy-start | bytes 100
  105.4 15.1 %copy-start.2 = (bf16[8,4,256]{2,1,0:T(4,128)(2,1)S(1)}, bf16[8,4,256]{2,1,0:T(4,128)(2,1)}, u32[]{:S(2)}) copy-start(bf16[8,4,256]{2,1,0:T(4,128)(2,1)} %param.16) | copy-start | bytes 49156
  105.4 15.1 %copy-start.4 = (bf16[8,32,128]{2,1,0:T(8,128)(2,1)S(1)}, bf16[8,32,128]{2,1,0:T(8,128)(2,1)}, u32[]{:S(2)}) copy-start(bf16[8,32,128]{2,1,0:T(8,128)(2,1)} %param.14) | copy-start | bytes 196612
  119.4 1.6 %copy-start.1 = (bf16[8,128,4,256]{3,2,1,0:T(4,128)(2,1)S(1)}, bf16[8,128,4,256]{3,2,1,0:T(4,128)(2,1)}, u32[]{:S(2)}) copy-start(bf16[8,128,4,256]{3,2,1,0:T(4,128)(2,1)} %param.15) | copy-start | bytes 6291460
  119.4 3.1 %copy-start.6 = (u32[32]{0:T(128)S(1)}, u32[32]{0:T(128)}, u32[]{:S(2)}) copy-start(u32[32]{0:T(128)} %constant.42) | copy-start | bytes 388
Sparse Core Ops, SparseCore 0:
  119.5 24.0 all-reduce.2
where the time goes:
time: 157 us; the launch traced here: 155 us
  waiting for transfers between devices  69 us (44%)
  local copies, waits for them, and re-layouts  41.9 us (27%)
  matrix products  19.5 us (12%)
  between operations  14.9 us (9%)
  starting transfers between devices  7.26 us (5%)
  other arithmetic  2.72 us (2%)
    all_to_all x1, waiting for transfers between devices, local(): lax.all_to_all(outgoing, 'replica', split_axis=0, concat_axis=0, tiled=True)  50.3 us
    dot_general x1, local copies, waits for them, and re-layouts, local(): product = jnp.dot(flat, weight_flat, preferred_element_type=jnp.float32)  19.4 us
    unnamed x18, local copies, waits for them, and re-layouts  19.2 us
    unnamed x2, waiting for transfers between devices  18.7 us
    dot_general x1, matrix products, local(): product = jnp.dot(flat, weight_flat, preferred_element_type=jnp.float32)  13.9 us
    all_to_all x1, starting transfers between devices, local(): lax.all_to_all(outgoing, 'replica', split_axis=0, concat_axis=0, tiled=True)  7.23 us
  transfers between devices with their start and end apart: 2, of which 2 were waited for; matrix products, arithmetic and copies ran while one was open for 25% of the time, Pallas kernels for 0%

commit v1 on v0

v1 whole, which is shorter than its diff:
```python
import functools
import math

import jax
import jax.numpy as jnp
from jax import lax
from jax.experimental import pallas as pl
from jax.experimental.pallas import tpu as pltpu
from jax.sharding import PartitionSpec as P

MESH = pl.DeviceIdType.MESH
F32 = jnp.float32
BF16 = jnp.bfloat16


def project_kernel(kvh, group_rows, perm_ref, feat_ref, w_ref, out_ref, by_head, acc):
    step = pl.program_id(0)
    chunk = feat_ref.shape[1]
    width = w_ref.shape[1]
    tile = kvh * group_rows

    @pl.when(step == 0)
    def _():
        acc[...] = jnp.zeros_like(acc)

    perm = perm_ref[...]
    for g in range(chunk // group_rows):
        moved = jnp.dot(
            perm, w_ref[g * tile : (g + 1) * tile, :], preferred_element_type=F32
        ).astype(BF16)
        for h in range(kvh):
            by_head[h, g * group_rows : (g + 1) * group_rows, :] = moved[
                h * group_rows : (h + 1) * group_rows, :
            ]
    feat = feat_ref[...]
    for h in range(kvh):
        acc[:, h * width : (h + 1) * width] += jnp.dot(
            feat, by_head[h], preferred_element_type=F32
        )

    @pl.when(step == pl.num_programs(0) - 1)
    def _():
        n_ten, _, cols = out_ref.shape
        for t in range(n_ten):
            out_ref[t] = acc[:, t * cols : (t + 1) * cols].astype(BF16)


def project(feat, weight, n_ten):
    rows, depth = feat.shape
    kvh, width = weight.shape[1:]
    group_rows = 256 // kvh
    tile = kvh * group_rows
    chunk = depth
    for c in range(128, 385, 128):
        if depth % c == 0:
            chunk = c
    at = jnp.arange(tile, dtype=jnp.int32)
    source = (at % group_rows) * kvh + at // group_rows
    perm = (source[:, None] == at[None, :]).astype(BF16)
    cols = kvh * width // n_ten
    return pl.pallas_call(
        functools.partial(project_kernel, kvh, group_rows),
        grid=(depth // chunk,),
        in_specs=[
            pl.BlockSpec((tile, tile), lambda k: (0, 0)),
            pl.BlockSpec((rows, chunk), lambda k: (0, k)),
            pl.BlockSpec((chunk * kvh, width), lambda k: (k, 0)),
        ],
        out_specs=pl.BlockSpec((n_ten, rows, cols), lambda k: (0, 0, 0)),
        out_shape=jax.ShapeDtypeStruct((n_ten, rows, cols), BF16),
        scratch_shapes=[
            pltpu.VMEM((kvh, chunk, width), BF16),
            pltpu.VMEM((rows, kvh * width), F32),
        ],
        compiler_params=pltpu.CompilerParams(vmem_limit_bytes=40 * 1024 * 1024),
        cost_estimate=pl.CostEstimate(
            flops=4 * rows * depth * kvh * width,
            bytes_accessed=2 * depth * (kvh * width + rows),
            transcendentals=0,
        ),
    )(perm, feat, weight.reshape(depth * kvh, width))


def attend_kernel(
    n_rep,
    n_ten,
    kvh,
    len_ref,
    part_ref,
    slot_ref,
    code_ref,
    cq_ref,
    sq_ref,
    cache_ref,
    fresh_ref,
    cross_ref,
    self_ref,
    got_t,
    outgoing,
    arrived,
    send_t,
    recv_t,
    send_r,
    recv_r,
):
    rep = lax.axis_index("replica")
    ten = lax.axis_index("tensor")
    reqs, heads, width = cq_ref.shape
    group = heads // kvh
    scale = 1.0 / math.sqrt(width)
    slot_rows = outgoing.shape[1]

    barrier = pltpu.get_barrier_semaphore()
    for d in range(1, n_ten):
        peer = lax.rem(ten + d, n_ten)
        pl.semaphore_signal(barrier, inc=1, device_id=(rep, peer), device_id_type=MESH)
    for d in range(1, n_rep):
        peer = lax.rem(rep + d, n_rep)
        pl.semaphore_signal(barrier, inc=1, device_id=(peer, ten), device_id_type=MESH)
    pl.semaphore_wait(barrier, n_ten + n_rep - 2)

    to_ten = []
    for d in range(1, n_ten):
        peer = lax.rem(ten + d, n_ten)
        copy = pltpu.make_async_remote_copy(
            src_ref=part_ref.at[peer],
            dst_ref=got_t.at[d - 1],
            send_sem=send_t.at[d - 1],
            recv_sem=recv_t.at[d - 1],
            device_id=(rep, peer),
            device_id_type=MESH,
        )
        copy.start()
        to_ten.append(copy)
    rows = part_ref.shape[1]
    at = lax.broadcasted_iota(jnp.int32, (n_rep * slot_rows, rows), 0)
    placing = (at == slot_ref[...]).astype(BF16)
    kv = part_ref[ten].astype(F32)
    for d in range(1, n_ten):
        to_ten[d - 1].wait_recv()
        kv = kv + got_t[d - 1].astype(F32)
    kv = kv.astype(BF16)
    placed = jnp.dot(placing, kv, preferred_element_type=F32)
    outgoing[...] = placed.reshape(outgoing.shape).astype(BF16)
    to_rep = []
    for d in range(1, n_rep):
        peer = lax.rem(rep + d, n_rep)
        copy = pltpu.make_async_remote_copy(
            src_ref=outgoing.at[peer],
            dst_ref=arrived.at[d],
            send_sem=send_r.at[d],
            recv_sem=recv_r.at[d],
            device_id=(peer, ten),
            device_id_type=MESH,
        )
        copy.start()
        to_rep.append(copy)
    arrived[0] = outgoing[rep]

    places = cache_ref.shape[1]
    col = lax.broadcasted_iota(jnp.int32, (heads, places), 1)
    row = lax.broadcasted_iota(jnp.int32, (heads, places), 0)
    same_head = lax.rem(col, kvh) == row // group
    for b in range(reqs):
        query = sq_ref[b]
        keys = cache_ref[b, :, :width]
        values = cache_ref[b, :, width:]
        score = (
            lax.dot_general(query, keys, (((1,), (1,)), ((), ())), preferred_element_type=F32)
            * scale
        )
        live = same_head & (col // kvh < len_ref[b])
        weight = jnp.where(live, jnp.exp(score), 0.0)
        fresh = fresh_ref[b].astype(F32)
        fresh_weight = jnp.exp(
            jnp.sum(query.astype(F32) * fresh[:, :width], axis=1, keepdims=True) * scale
        )
        total = jnp.sum(weight, axis=1, keepdims=True) + fresh_weight
        numer = jnp.dot(weight.astype(BF16), values, preferred_element_type=F32)
        numer = numer + fresh_weight.astype(BF16).astype(F32) * fresh[:, width:]
        self_ref[b] = (numer / total).astype(BF16)

    cross_query = cq_ref[...].astype(F32)
    queries = [
        cross_query[:, h * group : (h + 1) * group, :].reshape(reqs * group, width).astype(BF16)
        for h in range(kvh)
    ]
    total = [jnp.zeros((reqs * group, 1), F32)] * kvh
    numer = [jnp.zeros((reqs * group, width), F32)] * kvh
    batch = max(1, 128 // slot_rows)
    batch = min(batch, n_rep)
    count = jnp.zeros((reqs * group, 1), F32)
    for first in range(0, n_rep, batch):
        for d in range(max(1, first), first + batch):
            to_rep[d - 1].wait_recv()
        size = batch * slot_rows
        code = code_ref[:, first * slot_rows : first * slot_rows + size]
        owner_row = lax.broadcasted_iota(jnp.int32, (reqs * group, size), 0) // group
        mask = owner_row == code
        count = count + jnp.sum(mask.astype(F32), axis=1, keepdims=True)
        for h in range(kvh):
            both = arrived[first : first + batch, :, h * 2 * width : (h + 1) * 2 * width]
            both = both.astype(F32).reshape(size, 2 * width)
            raw = both[:, :width]
            keys = (
                raw * lax.rsqrt(jnp.mean(raw * raw, axis=1, keepdims=True) + 1e-05)
            ).astype(BF16)
            values = both[:, width:].astype(BF16)
            score = (
                lax.dot_general(
                    queries[h], keys, (((1,), (1,)), ((), ())), preferred_element_type=F32
                )
                * scale
            )
            weight = jnp.where(mask, jnp.exp(score), 0.0)
            total[h] = total[h] + jnp.sum(weight, axis=1, keepdims=True)
            numer[h] = numer[h] + jnp.dot(
                weight.astype(BF16), values, preferred_element_type=F32
            )
    has = count > 0.0
    parts = []
    for h in range(kvh):
        safe = jnp.where(has, total[h], 1.0)
        parts.append(jnp.where(has, numer[h] / safe, 0.0).reshape(reqs, group, width))
    cross_ref[...] = jnp.concatenate(parts, axis=1).astype(BF16)

    for copy in to_ten:
        copy.wait_send()
    for copy in to_rep:
        copy.wait_send()


def local(
    n_rep,
    n_ten,
    features,
    kv_weight,
    image_owner,
    image_request,
    cross_query,
    self_query,
    self_cache,
    fresh_key_value,
    cache_len,
):
    me = lax.axis_index("replica")
    images, patches, depth = features.shape
    reqs, heads, width = cross_query.shape
    kvh = self_cache.shape[2]
    group = heads // kvh
    slot_cap = max(2, 2 * images // n_rep)
    rows = images * patches
    slot_rows = slot_cap * patches

    owners = image_owner.reshape(n_rep, images)
    requests = image_request.reshape(n_rep, images)
    mine = lax.dynamic_index_in_dim(owners, me, 0, keepdims=False)
    at = jnp.arange(images, dtype=jnp.int32)
    earlier = (mine[:, None] == mine[None, :]) & (at[:, None] > at[None, :])
    rank = jnp.sum(earlier.astype(jnp.int32), axis=1, dtype=jnp.int32)
    slot = mine * slot_cap + rank
    slot_row = (slot[:, None] * patches + jnp.arange(patches, dtype=jnp.int32)[None, :]).reshape(
        1, rows
    )

    source = lax.rem(me - jnp.arange(n_rep, dtype=jnp.int32) + n_rep, n_rep)
    from_owner = owners[source]
    match = from_owner == me
    before = (at[:, None] < at[None, :]).astype(BF16)
    place = jnp.dot(match.astype(BF16), before, preferred_element_type=F32).astype(jnp.int32)
    chosen = match[:, None, :] & (
        place[:, None, :] == jnp.arange(slot_cap, dtype=jnp.int32)[None, :, None]
    )
    code = jnp.sum(jnp.where(chosen, requests[source][:, None, :] + 1, 0), axis=-1) - 1
    code = jnp.broadcast_to(code[:, :, None], (n_rep, slot_cap, patches)).reshape(
        1, n_rep * slot_rows
    )

    part = project(features.reshape(rows, depth), kv_weight, n_ten)
    cache = self_cache.reshape(reqs, self_cache.shape[1] * kvh, 2 * width)
    fresh = jnp.broadcast_to(
        fresh_key_value[:, :, None, :], (reqs, kvh, group, 2 * width)
    ).reshape(reqs, heads, 2 * width)
    cols = kvh * 2 * width
    vmem = pl.BlockSpec(memory_space=pltpu.VMEM)
    return pl.pallas_call(
        functools.partial(attend_kernel, n_rep, n_ten, kvh),
        in_specs=[pl.BlockSpec(memory_space=pltpu.SMEM)] + [vmem] * 7,
        out_specs=(vmem, vmem),
        out_shape=(
            jax.ShapeDtypeStruct(cross_query.shape, BF16),
            jax.ShapeDtypeStruct(self_query.shape, BF16),
        ),
        scratch_shapes=[
            pltpu.VMEM((n_ten - 1, rows, cols), BF16),
            pltpu.VMEM((n_rep, slot_rows, cols), BF16),
            pltpu.VMEM((n_rep, slot_rows, cols), BF16),
            pltpu.SemaphoreType.DMA((n_ten - 1,)),
            pltpu.SemaphoreType.DMA((n_ten - 1,)),
            pltpu.SemaphoreType.DMA((n_rep,)),
            pltpu.SemaphoreType.DMA((n_rep,)),
        ],
        compiler_params=pltpu.CompilerParams(
            collective_id=0,
            has_side_effects=True,
            vmem_limit_bytes=40 * 1024 * 1024,
        ),
    )(cache_len, part, slot_row, code, cross_query, self_query, cache, fresh)


def solution(mesh):
    n_rep, n_ten = mesh.shape["replica"], mesh.shape["tensor"]
    return jax.shard_map(
        functools.partial(local, n_rep, n_ten),
        mesh=mesh,
        in_specs=(
            P("replica", None, "tensor"),
            P("tensor", None, None),
            P(),
            P(),
            P("replica", "tensor", None),
            P("replica", "tensor", None),
            P("replica", None, "tensor", None),
            P("replica", "tensor", None),
            P("replica"),
        ),
        out_specs=(P("replica", "tensor", None), P("replica", "tensor", None)),
        check_vma=False,
    )
```

time: 157 us -> 59.2 us (0.38)
  the two profiles are of different devices: /device:TPU:8 before, /device:TPU:31 now
where the time goes in v1:
time: 59.2 us; the launch traced here: 58.7 us
  Pallas kernels  47.2 us (80%)
  local copies, waits for them, and re-layouts  9.86 us (17%)
  between operations  0.8 us (1%)
  other arithmetic  0.75 us (1%)
    pallas_call x1, Pallas kernels, local(): pl.pallas_call(functools.partial(attend_kernel, n_rep, n_ten, kvh), in_sp...  32.7 us
    pallas_call x1, Pallas kernels, project(): pl.pallas_call(functools.partial(project_kernel, kvh, group_rows), grid=(...  14.5 us
    reshape x1, local copies, waits for them, and re-layouts, local(): part = project(features.reshape(rows, depth), kv_weight, n_ten)  3.02 us
    reshape x1, local copies, waits for them, and re-layouts, local(): cache = self_cache.reshape(reqs, self_cache.shape[1] * kvh, 2 * width)  2.59 us
    unnamed x10, local copies, waits for them, and re-layouts  1.29 us

profile of v1, /device:TPU:31, one launch (start us, length us, event | category | flops | bytes accessed | tf_op | source)
XLA Modules:
  0.0 58.7 jit_solution(8090346563948907462)
XLA Ops:
  0.6 0.0 copy-start
  0.7 0.8 %reshape.133 = s32[16,64]{1,0:T(8,128)S(1)} reshape(s32[1024]{0:T(1024)} %param.11) | data formatting | bytes 8192 | tf_op jit(solution)/shard_map/reshape | solution.py:255
  1.5 0.2 convert_reduce_fusion
  1.7 0.6 gather_fusion
  2.2 0.1 convolution_convert_fusion
  2.4 0.8 %reshape.134 = s32[16,64]{1,0:T(8,128)S(1)} reshape(s32[1024]{0:T(1024)} %param.12) | data formatting | bytes 8192 | tf_op jit(solution)/shard_map/reshape | solution.py:256
  3.1 0.6 gather_fusion.1
  3.7 0.3 select_reduce_fusion
  4.1 0.1 iota_add_fusion
  4.1 0.1 add.100.slot_ref
  4.2 0.1 broadcast_in_dim.14
  4.3 0.1 reshape.135.code_ref
  4.4 0.1 fusion.perm_ref
  4.5 0.0 copy-done
  4.6 3.0 %reshape.131.feat_ref = bf16[256,3840]{1,0:T(8,128)(2,1)S(1)} reshape(bf16[64,4,3840]{2,1,0:T(4,128)(2,1)} %param.9) | data formatting | bytes 3932160 | tf_op jit(solution)/shard_map/reshape | solution.py:279
  7.6 14.5 %shard_map.104.part_ref = bf16[2,256,1024]{2,1,0:T(8,128)(2,1)S(1)} custom-call(bf16[256,256]{1,0:T(8,128)(2,1)S(1)} %fusion.perm_ref, bf16[256,3840]{1,0:T(8,128)(2,1)S(1)} %reshape.131.feat_ref, bf16[30720,256]{1,0:T(8,128)(2,1)} %bitcast.10), custom_call_target="tpu_custom_call" | custom-call | flops 8053063680 | bytes 17694720 | tf_op jit(solution)/shard_map/pallas_call | solution.py:61
  22.1 0.0 copy-start.1
  22.1 0.0 copy-start.2
  22.1 0.0 copy-start.3
  22.1 2.6 %reshape.136.cache_ref = bf16[8,512,256]{2,1,0:T(8,128)(2,1)S(1)} reshape(bf16[8,128,4,256]{3,2,1,0:T(4,128)(2,1)} %param.15) | data formatting | bytes 4194304 | tf_op jit(solution)/shard_map/reshape | solution.py:280
  24.7 0.0 copy-done.1
  24.7 0.0 copy-done.2
  24.8 0.0 copy-done.3
  24.8 32.7 %shard_map.105 = (bf16[8,32,128]{2,1,0:T(8,128)(2,1)S(1)}, bf16[8,32,128]{2,1,0:T(8,128)(2,1)S(1)}) custom-call(s32[8]{0:T(128)S(1)} %copy-done.3, bf16[2,256,1024]{2,1,0:T(8,128)(2,1)S(1)} %shard_map.104.part_ref, s32[1,256]{1,0:T(1,128)S(1)} %add.100.slot_ref, s32[1,512]{1,0:T(1,128)S(1)} %reshape.135.code_ref, bf16[8,32,128]{2,1,0:T(8,128)(2,1)S(1)} %copy-done.1, ...), custom_call_target="tpu_custom_call" | custom-call | tf_op jit(solution)/shard_map/pallas_call | solution.py:286
  57.5 0.6 %copy.13 = bf16[8,32,128]{2,1,0:T(8,128)(2,1)} copy(bf16[8,32,128]{2,1,0:T(8,128)(2,1)S(1)} %get-tuple-element.4) | data formatting | bytes 131072
  58.1 0.6 %copy.14 = bf16[8,32,128]{2,1,0:T(8,128)(2,1)} copy(bf16[8,32,128]{2,1,0:T(8,128)(2,1)S(1)} %get-tuple-element.5) | data formatting | bytes 131072
  (9 shorter events, 0.1 us)
Async XLA Ops:
  0.6 3.9 %copy-start = (bf16[8,4,256]{2,1,0:T(4,128)(2,1)S(1)}, bf16[8,4,256]{2,1,0:T(4,128)(2,1)}, u32[]{:S(2)}) copy-start(bf16[8,4,256]{2,1,0:T(4,128)(2,1)} %param.16) | copy-start | bytes 49156
  22.1 2.6 %copy-start.1 = (bf16[8,32,128]{2,1,0:T(8,128)(2,1)S(1)}, bf16[8,32,128]{2,1,0:T(8,128)(2,1)}, u32[]{:S(2)}) copy-start(bf16[8,32,128]{2,1,0:T(8,128)(2,1)} %cq_ref.1) | copy-start | bytes 196612
  22.1 2.6 %copy-start.2 = (bf16[8,32,128]{2,1,0:T(8,128)(2,1)S(1)}, bf16[8,32,128]{2,1,0:T(8,128)(2,1)}, u32[]{:S(2)}) copy-start(bf16[8,32,128]{2,1,0:T(8,128)(2,1)} %sq_ref.1) | copy-start | bytes 196612
  22.1 2.6 %copy-start.3 = (s32[8]{0:T(128)S(1)}, s32[8]{0:T(128)}, u32[]{:S(2)}) copy-start(s32[8]{0:T(128)} %len_ref.1) | copy-start | bytes 100

commit v2 on v1

v2 whole, which is shorter than its diff:
```python
import functools
import math

import jax
import jax.numpy as jnp
from jax import lax
from jax.experimental import pallas as pl
from jax.experimental.pallas import tpu as pltpu
from jax.sharding import PartitionSpec as P

MESH = pl.DeviceIdType.MESH
F32 = jnp.float32
BF16 = jnp.bfloat16


def step_kernel(
    n_rep,
    n_ten,
    kvh_all,
    kvh,
    len_ref,
    slot_ref,
    code_ref,
    perm_ref,
    feat_ref,
    w_ref,
    cq_ref,
    sq_ref,
    cache_hbm,
    fresh_ref,
    cross_ref,
    self_ref,
    feat,
    by_head,
    acc,
    part,
    got,
    outgoing,
    arrived,
    weights,
    cache_ref,
    cache_sem,
    send_t,
    recv_t,
    send_r,
    recv_r,
):
    rep = lax.axis_index("replica")
    ten = lax.axis_index("tensor")
    half = pl.program_id(0)
    step = pl.program_id(1)
    steps = pl.num_programs(1)
    reqs, heads, width = cq_ref.shape
    group = heads // kvh
    scale = 1.0 / math.sqrt(width)
    slot_rows = outgoing.shape[2]
    cols = kvh * width
    rows, chunk = feat.shape[1:]
    run = 256 // kvh_all
    tile = run * kvh_all
    cache_copy = pltpu.make_async_copy(cache_hbm, cache_ref, cache_sem)

    def to_ten(which, d):
        peer = lax.rem(ten + d, n_ten)
        return pltpu.make_async_remote_copy(
            src_ref=part.at[which, peer],
            dst_ref=got.at[which, d - 1],
            send_sem=send_t.at[which, d - 1],
            recv_sem=recv_t.at[which, d - 1],
            device_id=(rep, peer),
            device_id_type=MESH,
        )

    def to_rep(which, d):
        peer = lax.rem(rep + d, n_rep)
        return pltpu.make_async_remote_copy(
            src_ref=outgoing.at[which, peer],
            dst_ref=arrived.at[which, d],
            send_sem=send_r.at[which, d],
            recv_sem=recv_r.at[which, d],
            device_id=(peer, ten),
            device_id_type=MESH,
        )

    def route(which):
        at = lax.broadcasted_iota(jnp.int32, (n_rep * slot_rows, rows), 0)
        placing = (at == slot_ref[...]).astype(BF16)
        kv = part[which, ten].astype(F32)
        for d in range(1, n_ten):
            to_ten(which, d).wait_recv()
            kv = kv + got[which, d - 1].astype(F32)
        placed = jnp.dot(placing, kv.astype(BF16), preferred_element_type=F32)
        outgoing[which] = placed.reshape(n_rep, slot_rows, cols).astype(BF16)
        for d in range(1, n_rep):
            to_rep(which, d).start()
        arrived[which, 0] = outgoing[which, rep]

    @pl.when((half == 0) & (step == 0))
    def _():
        barrier = pltpu.get_barrier_semaphore()
        for d in range(1, n_ten):
            peer = lax.rem(ten + d, n_ten)
            pl.semaphore_signal(barrier, inc=1, device_id=(rep, peer), device_id_type=MESH)
        for d in range(1, n_rep):
            peer = lax.rem(rep + d, n_rep)
            pl.semaphore_signal(barrier, inc=1, device_id=(peer, ten), device_id_type=MESH)
        cache_copy.start()

    @pl.when(half == 0)
    def _():
        feat[step] = feat_ref[...].astype(F32).reshape(rows, chunk).astype(BF16)

    @pl.when(step == 0)
    def _():
        acc[...] = jnp.zeros_like(acc)

    perm = perm_ref[...]
    for g in range(0, chunk // run, 2):
        two = jnp.concatenate(
            [w_ref[g * tile : (g + 1) * tile, :], w_ref[(g + 1) * tile : (g + 2) * tile, :]],
            axis=1,
        )
        moved = jnp.dot(perm, two, preferred_element_type=F32).astype(BF16)
        for h in range(kvh_all):
            lanes = (h % 2) * width
            for q in range(2):
                by_head[
                    h // 2, (g + q) * run : (g + q + 1) * run, lanes : lanes + width
                ] = moved[h * run : (h + 1) * run, q * width : (q + 1) * width]
    now = feat[step]
    for p in range(kvh_all // 2):
        acc[:, p * 2 * width : (p + 1) * 2 * width] += jnp.dot(
            now, by_head[p], preferred_element_type=F32
        )

    @pl.when(step == steps - 1)
    def _():
        for t in range(n_ten):
            part[half, t] = acc[:, t * cols : (t + 1) * cols].astype(BF16)

    @pl.when((half == 0) & (step == steps - 1))
    def _():
        pl.semaphore_wait(pltpu.get_barrier_semaphore(), n_ten + n_rep - 2)
        for d in range(1, n_ten):
            to_ten(0, d).start()

    @pl.when((half == 1) & (step == jnp.minimum(1, steps - 1)))
    def _():
        route(0)

    @pl.when((half == 1) & (step == steps - 1))
    def _():
        for d in range(1, n_ten):
            to_ten(1, d).start()
        route(1)

        cache_copy.wait()
        places = cache_ref.shape[1] * kvh
        col = lax.broadcasted_iota(jnp.int32, (heads, places), 1)
        row = lax.broadcasted_iota(jnp.int32, (heads, places), 0)
        same_head = lax.rem(col, kvh) == row // group
        for b in range(reqs):
            query = sq_ref[b]
            both = cache_ref[b].astype(F32).reshape(places, 2 * width).astype(BF16)
            score = (
                lax.dot_general(
                    query, both[:, :width], (((1,), (1,)), ((), ())), preferred_element_type=F32
                )
                * scale
            )
            live = same_head & (col // kvh < len_ref[b])
            weight = jnp.where(live, jnp.exp(score), 0.0)
            fresh = fresh_ref[b].astype(F32)
            fresh_weight = jnp.exp(
                jnp.sum(query.astype(F32) * fresh[:, :width], axis=1, keepdims=True) * scale
            )
            total = jnp.sum(weight, axis=1, keepdims=True) + fresh_weight
            numer = jnp.dot(
                weight.astype(BF16), both[:, width:], preferred_element_type=F32
            )
            numer = numer + fresh_weight.astype(BF16).astype(F32) * fresh[:, width:]
            self_ref[b] = (numer / total).astype(BF16)

        cross_query = cq_ref[...].astype(F32)
        size = n_rep * slot_rows
        owner_row = lax.broadcasted_iota(jnp.int32, (reqs * group, size), 0) // group
        mask = owner_row == code_ref[...]
        has = jnp.sum(mask.astype(F32), axis=1, keepdims=True) > 0.0
        for d in range(1, n_rep):
            to_rep(0, d).wait_recv()
        safe = []
        for h in range(kvh):
            query = cross_query[:, h * group : (h + 1) * group, :]
            query = query.reshape(reqs * group, width).astype(BF16)
            raw = arrived[0, :, :, h * width : (h + 1) * width].astype(F32).reshape(size, width)
            keys = (
                raw * lax.rsqrt(jnp.mean(raw * raw, axis=1, keepdims=True) + 1e-05)
            ).astype(BF16)
            score = (
                lax.dot_general(
                    query, keys, (((1,), (1,)), ((), ())), preferred_element_type=F32
                )
                * scale
            )
            weight = jnp.where(mask, jnp.exp(score), 0.0)
            safe.append(jnp.where(has, jnp.sum(weight, axis=1, keepdims=True), 1.0))
            weights[h] = weight.astype(BF16)
        for d in range(1, n_rep):
            to_rep(1, d).wait_recv()
        parts = []
        for h in range(kvh):
            values = arrived[1, :, :, h * width : (h + 1) * width]
            values = values.astype(F32).reshape(size, width).astype(BF16)
            numer = jnp.dot(weights[h], values, preferred_element_type=F32)
            parts.append(jnp.where(has, numer / safe[h], 0.0).reshape(reqs, group, width))
        cross_ref[...] = jnp.concatenate(parts, axis=1).astype(BF16)

        for which in range(2):
            for d in range(1, n_ten):
                to_ten(which, d).wait_send()
            for d in range(1, n_rep):
                to_rep(which, d).wait_send()


def local(
    n_rep,
    n_ten,
    features,
    kv_weight,
    image_owner,
    image_request,
    cross_query,
    self_query,
    self_cache,
    fresh_key_value,
    cache_len,
):
    me = lax.axis_index("replica")
    images, patches, depth = features.shape
    reqs, heads, width = cross_query.shape
    kvh = self_cache.shape[2]
    kvh_all = kv_weight.shape[1]
    group = heads // kvh
    slot_cap = max(2, 2 * images // n_rep)
    rows = images * patches
    slot_rows = slot_cap * patches

    ids = (image_owner * reqs + image_request).reshape(n_rep, images)
    owners = ids // reqs
    mine = lax.dynamic_index_in_dim(ids, me, 0, keepdims=False) // reqs
    at = jnp.arange(images, dtype=jnp.int32)
    earlier = (mine[:, None] == mine[None, :]) & (at[:, None] > at[None, :])
    rank = jnp.sum(earlier.astype(jnp.int32), axis=1, dtype=jnp.int32)
    slot = mine * slot_cap + rank
    slot_row = (slot[:, None] * patches + jnp.arange(patches, dtype=jnp.int32)[None, :]).reshape(
        1, rows
    )

    match = owners == me
    before = (at[:, None] < at[None, :]).astype(BF16)
    place = jnp.dot(match.astype(BF16), before, preferred_element_type=F32).astype(jnp.int32)
    chosen = match[:, None, :] & (
        place[:, None, :] == jnp.arange(slot_cap, dtype=jnp.int32)[None, :, None]
    )
    code = jnp.sum(jnp.where(chosen, (ids - me * reqs)[:, None, :] + 1, 0), axis=-1) - 1
    source = lax.rem(me - jnp.arange(n_rep, dtype=jnp.int32) + n_rep, n_rep)
    turn = source[:, None] == jnp.arange(n_rep, dtype=jnp.int32)[None, :]
    code = jnp.sum(jnp.where(turn[:, :, None], code[None], 0), axis=1)
    code = jnp.broadcast_to(code[:, :, None], (n_rep, slot_cap, patches)).reshape(
        1, n_rep * slot_rows
    )

    tile = 256 // kvh_all * kvh_all
    spot = jnp.arange(tile, dtype=jnp.int32)
    origin = (spot % (tile // kvh_all)) * kvh_all + spot // (tile // kvh_all)
    perm = (origin[:, None] == spot[None, :]).astype(BF16)
    fresh = jnp.broadcast_to(
        fresh_key_value[:, :, None, :], (reqs, kvh, group, 2 * width)
    ).reshape(reqs, heads, 2 * width)
    chunk = depth
    for c in range(128, 385, 128):
        if depth % c == 0:
            chunk = c
    steps = depth // chunk
    cols = kvh * width
    vmem = pl.BlockSpec(memory_space=pltpu.VMEM)
    return pl.pallas_call(
        functools.partial(step_kernel, n_rep, n_ten, kvh_all, kvh),
        grid=(2, steps),
        in_specs=[
            pl.BlockSpec(memory_space=pltpu.SMEM),
            vmem,
            vmem,
            vmem,
            pl.BlockSpec(
                (images, patches, chunk), lambda j, k: (0, 0, k * (1 - j) + (steps - 1) * j)
            ),
            pl.BlockSpec((chunk * kvh_all, width), lambda j, k: (k, j)),
            vmem,
            vmem,
            pl.BlockSpec(memory_space=pl.ANY),
            vmem,
        ],
        out_specs=(vmem, vmem),
        out_shape=(
            jax.ShapeDtypeStruct(cross_query.shape, BF16),
            jax.ShapeDtypeStruct(self_query.shape, BF16),
        ),
        scratch_shapes=[
            pltpu.VMEM((steps, rows, chunk), BF16),
            pltpu.VMEM((kvh_all // 2, chunk, 2 * width), BF16),
            pltpu.VMEM((rows, kvh_all * width), F32),
            pltpu.VMEM((2, n_ten, rows, cols), BF16),
            pltpu.VMEM((2, n_ten - 1, rows, cols), BF16),
            pltpu.VMEM((2, n_rep, slot_rows, cols), BF16),
            pltpu.VMEM((2, n_rep, slot_rows, cols), BF16),
            pltpu.VMEM((kvh, reqs * group, n_rep * slot_rows), BF16),
            pltpu.VMEM(self_cache.shape, BF16),
            pltpu.SemaphoreType.DMA,
            pltpu.SemaphoreType.DMA((2, n_ten - 1)),
            pltpu.SemaphoreType.DMA((2, n_ten - 1)),
            pltpu.SemaphoreType.DMA((2, n_rep)),
            pltpu.SemaphoreType.DMA((2, n_rep)),
        ],
        compiler_params=pltpu.CompilerParams(
            collective_id=0,
            has_side_effects=True,
            vmem_limit_bytes=48 * 1024 * 1024,
        ),
    )(
        cache_len,
        slot_row,
        code,
        perm,
        features,
        kv_weight.reshape(depth * kvh_all, 2 * width),
        cross_query,
        self_query,
        self_cache,
        fresh,
    )


def solution(mesh):
    n_rep, n_ten = mesh.shape["replica"], mesh.shape["tensor"]
    return jax.shard_map(
        functools.partial(local, n_rep, n_ten),
        mesh=mesh,
        in_specs=(
            P("replica", None, "tensor"),
            P("tensor", None, None),
            P(),
            P(),
            P("replica", "tensor", None),
            P("replica", "tensor", None),
            P("replica", None, "tensor", None),
            P("replica", "tensor", None),
            P("replica"),
        ),
        out_specs=(P("replica", "tensor", None), P("replica", "tensor", None)),
        check_vma=False,
    )
```

time: 59.2 us -> 50.7 us (0.86)
  the two profiles are of different devices: /device:TPU:31 before, /device:TPU:8 now
where the time goes in v2:
time: 50.7 us; the launch traced here: 50 us
  Pallas kernels  40 us (79%)
  local copies, waits for them, and re-layouts  7.19 us (14%)
  other arithmetic  1.94 us (4%)
  between operations  0.74 us (1%)
    pallas_call x1, Pallas kernels, local(): pl.pallas_call(functools.partial(step_kernel, n_rep, n_ten, kvh_all, kvh)...  40 us
    unnamed x14, local copies, waits for them, and re-layouts  6.73 us

profile of v2, /device:TPU:8, one launch (start us, length us, event | category | flops | bytes accessed | tf_op | source)
XLA Modules:
  0.0 50.0 jit_solution(16267649600367474402)
XLA Ops:
  0.6 0.0 copy-start
  0.7 0.1 iota_compare_fusion.5
  0.7 0.7 %multiply_add_fusion = s32[1024]{0:T(1024)S(1)} fusion(s32[1024]{0:T(1024)} %param.12, s32[1024]{0:T(1024)} %param.11), kind=kLoop, calls=%fused_computation.23 | loop fusion | flops 2048 | bytes 12288 | tf_op jit(solution)/shard_map/add | solution.py:248
  1.5 0.1 reshape.177
  1.6 0.2 convert_reduce_fusion
  1.8 0.1 convolution_convert_fusion
  1.9 0.4 select_reduce_fusion.1
  2.3 0.1 copy.12
  2.4 0.4 select_reduce_fusion
  2.7 0.1 iota_add_fusion
  2.8 0.1 add.100.slot_ref
  2.9 0.1 broadcast_in_dim.41
  3.0 0.1 reshape.178.code_ref
  3.1 0.1 fusion.perm_ref
  3.2 0.0 copy-done
  3.3 0.0 copy-start.1
  3.3 1.6 %copy-done.1 = bf16[8,128,4,256]{3,2,1,0:T(4,128)(2,1)S(1)} copy-done((bf16[8,128,4,256]{3,2,1,0:T(4,128)(2,1)S(1)}, bf16[8,128,4,256]{3,2,1,0:T(4,128)(2,1)}, u32[]{:S(2)}) %copy-start.1) | copy-done | bytes 2097176
  4.9 0.0 copy-start.2
  4.9 1.5 %copy-done.2 = bf16[64,4,3840]{2,1,0:T(4,128)(2,1)S(1)} copy-done((bf16[64,4,3840]{2,1,0:T(4,128)(2,1)S(1)}, bf16[64,4,3840]{2,1,0:T(4,128)(2,1)}, u32[]{:S(2)}) %copy-start.2) | copy-done | bytes 1966104
  6.4 0.0 copy-start.3
  6.4 0.8 %copy-done.3 = bf16[8,32,128]{2,1,0:T(8,128)(2,1)S(1)} copy-done((bf16[8,32,128]{2,1,0:T(8,128)(2,1)S(1)}, bf16[8,32,128]{2,1,0:T(8,128)(2,1)}, u32[]{:S(2)}) %copy-start.3) | copy-done | bytes 65560
  7.2 0.0 copy-start.4
  7.2 0.8 %copy-done.4 = bf16[8,32,128]{2,1,0:T(8,128)(2,1)S(1)} copy-done((bf16[8,32,128]{2,1,0:T(8,128)(2,1)S(1)}, bf16[8,32,128]{2,1,0:T(8,128)(2,1)}, u32[]{:S(2)}) %copy-start.4) | copy-done | bytes 65560
  8.1 0.0 copy-start.5
  8.1 0.7 %copy-done.5 = s32[8]{0:T(128)S(1)} copy-done((s32[8]{0:T(128)S(1)}, s32[8]{0:T(128)}, u32[]{:S(2)}) %copy-start.5) | copy-done | bytes 56
  8.7 40.0 %shard_map.104 = (bf16[8,32,128]{2,1,0:T(8,128)(2,1)S(1)}, bf16[8,32,128]{2,1,0:T(8,128)(2,1)S(1)}) custom-call(s32[8]{0:T(128)S(1)} %copy-done.5, s32[1,256]{1,0:T(1,128)S(1)} %add.100.slot_ref, s32[1,512]{1,0:T(1,128)S(1)} %reshape.178.code_ref, bf16[256,256]{1,0:T(8,128)(2,1)S(1)} %fusion.perm_ref, bf16[64,4,3840]{2,1,0:T(4,128)(2,1)S(1)} %copy-done.2, ...), custom_call_target="tpu_custom_call" | custom-call | tf_op jit(solution)/shard_map/pallas_call | solution.py:287
  48.7 0.6 %copy.15 = bf16[8,32,128]{2,1,0:T(8,128)(2,1)} copy(bf16[8,32,128]{2,1,0:T(8,128)(2,1)S(1)} %get-tuple-element.4) | data formatting | bytes 131072
  49.4 0.6 %copy.16 = bf16[8,32,128]{2,1,0:T(8,128)(2,1)} copy(bf16[8,32,128]{2,1,0:T(8,128)(2,1)S(1)} %get-tuple-element.5) | data formatting | bytes 131072
  (9 shorter events, 0.1 us)
Async XLA Ops:
  0.6 2.6 %copy-start = (bf16[8,4,256]{2,1,0:T(4,128)(2,1)S(1)}, bf16[8,4,256]{2,1,0:T(4,128)(2,1)}, u32[]{:S(2)}) copy-start(bf16[8,4,256]{2,1,0:T(4,128)(2,1)} %param.16) | copy-start | bytes 49156
  3.3 1.6 %copy-start.1 = (bf16[8,128,4,256]{3,2,1,0:T(4,128)(2,1)S(1)}, bf16[8,128,4,256]{3,2,1,0:T(4,128)(2,1)}, u32[]{:S(2)}) copy-start(bf16[8,128,4,256]{3,2,1,0:T(4,128)(2,1)} %cache_hbm.1) | copy-start | bytes 6291460
  4.9 1.5 %copy-start.2 = (bf16[64,4,3840]{2,1,0:T(4,128)(2,1)S(1)}, bf16[64,4,3840]{2,1,0:T(4,128)(2,1)}, u32[]{:S(2)}) copy-start(bf16[64,4,3840]{2,1,0:T(4,128)(2,1)} %feat_ref.1) | copy-start | bytes 5898244
  6.4 0.8 %copy-start.3 = (bf16[8,32,128]{2,1,0:T(8,128)(2,1)S(1)}, bf16[8,32,128]{2,1,0:T(8,128)(2,1)}, u32[]{:S(2)}) copy-start(bf16[8,32,128]{2,1,0:T(8,128)(2,1)} %cq_ref.1) | copy-start | bytes 196612
  7.2 0.8 %copy-start.4 = (bf16[8,32,128]{2,1,0:T(8,128)(2,1)S(1)}, bf16[8,32,128]{2,1,0:T(8,128)(2,1)}, u32[]{:S(2)}) copy-start(bf16[8,32,128]{2,1,0:T(8,128)(2,1)} %sq_ref.1) | copy-start | bytes 196612
  8.1 0.7 %copy-start.5 = (s32[8]{0:T(128)S(1)}, s32[8]{0:T(128)}, u32[]{:S(2)}) copy-start(s32[8]{0:T(128)} %len_ref.1) | copy-start | bytes 100

commit v3 on v2

--- a/solution.py
+++ b/solution.py
@@ -75,12 +75,23 @@
         peer = lax.rem(rep + d, n_rep)
         return pltpu.make_async_remote_copy(
             src_ref=outgoing.at[which, peer],
-            dst_ref=arrived.at[which, d],
+            dst_ref=arrived.at[which, rep],
             send_sem=send_r.at[which, d],
-            recv_sem=recv_r.at[which, d],
+            recv_sem=recv_r.at[which, rep],
             device_id=(peer, ten),
             device_id_type=MESH,
         )
+
+    def wait_arrival(which, d):
+        source = lax.rem(rep - d + n_rep, n_rep)
+        pltpu.make_async_remote_copy(
+            src_ref=outgoing.at[which, source],
+            dst_ref=arrived.at[which, source],
+            send_sem=send_r.at[which, d],
+            recv_sem=recv_r.at[which, source],
+            device_id=(source, ten),
+            device_id_type=MESH,
+        ).wait_recv()
 
     def route(which):
         at = lax.broadcasted_iota(jnp.int32, (n_rep * slot_rows, rows), 0)
@@ -93,7 +104,7 @@
         outgoing[which] = placed.reshape(n_rep, slot_rows, cols).astype(BF16)
         for d in range(1, n_rep):
             to_rep(which, d).start()
-        arrived[which, 0] = outgoing[which, rep]
+        arrived[which, rep] = outgoing[which, rep]
 
     @pl.when((half == 0) & (step == 0))
     def _():
@@ -187,7 +198,7 @@
         mask = owner_row == code_ref[...]
         has = jnp.sum(mask.astype(F32), axis=1, keepdims=True) > 0.0
         for d in range(1, n_rep):
-            to_rep(0, d).wait_recv()
+            wait_arrival(0, d)
         safe = []
         for h in range(kvh):
             query = cross_query[:, h * group : (h + 1) * group, :]
@@ -206,7 +217,7 @@
             safe.append(jnp.where(has, jnp.sum(weight, axis=1, keepdims=True), 1.0))
             weights[h] = weight.astype(BF16)
         for d in range(1, n_rep):
-            to_rep(1, d).wait_recv()
+            wait_arrival(1, d)
         parts = []
         for h in range(kvh):
             values = arrived[1, :, :, h * width : (h + 1) * width]
@@ -263,9 +274,6 @@
         place[:, None, :] == jnp.arange(slot_cap, dtype=jnp.int32)[None, :, None]
     )
     code = jnp.sum(jnp.where(chosen, (ids - me * reqs)[:, None, :] + 1, 0), axis=-1) - 1
-    source = lax.rem(me - jnp.arange(n_rep, dtype=jnp.int32) + n_rep, n_rep)
-    turn = source[:, None] == jnp.arange(n_rep, dtype=jnp.int32)[None, :]
-    code = jnp.sum(jnp.where(turn[:, :, None], code[None], 0), axis=1)
     code = jnp.broadcast_to(code[:, :, None], (n_rep, slot_cap, patches)).reshape(
         1, n_rep * slot_rows
     )
@@ -278,7 +286,7 @@
         fresh_key_value[:, :, None, :], (reqs, kvh, group, 2 * width)
     ).reshape(reqs, heads, 2 * width)
     chunk = depth
-    for c in range(128, 385, 128):
+    for c in range(256, 769, 256):
         if depth % c == 0:
             chunk = c
     steps = depth // chunk
@@ -325,7 +333,7 @@
         compiler_params=pltpu.CompilerParams(
             collective_id=0,
             has_side_effects=True,
-            vmem_limit_bytes=48 * 1024 * 1024,
+            vmem_limit_bytes=60 * 1024 * 1024,
         ),
     )(
         cache_len,

time: 50.7 us -> 46.7 us (0.921)
  local copies, waits for them, and re-layouts: 7.19 us -> 5.14 us
  Pallas kernels: 40 us -> 38.3 us
    unnamed x14 -> x4, local copies, waits for them, and re-layouts: 6.73 us -> 2.96 us
    pallas_call x1, Pallas kernels: 40 us -> 38.3 us  [local(): pl.pallas_call(functools.partial(step_kernel, n_rep, n_ten, kvh_all, kvh)...]
    reshape x1, local copies, waits for them, and re-layouts: 0.02 us -> 0.67 us  [local(): fresh = jnp.broadcast_to(fresh_key_value[:, :, None, :], (reqs, kvh, grou...]
    convert_element_type x1, other arithmetic: 0.1 us -> 0.74 us  [local(): perm = (origin[:, None] == spot[None, :]).astype(BF16)]
    reshape x1, local copies, waits for them, and re-layouts: 0.12 us -> 0.7 us  [local(): jnp.broadcast_to(code[:, :, None], (n_rep, slot_cap, patches))]
    add x1, local copies, waits for them, and re-layouts: 0.11 us -> 0.68 us  [local(): slot[:, None] * patches + jnp.arange(patches, dtype=jnp.int32)[None, :]]
where the time goes in v3:
time: 46.7 us; the launch traced here: 46.4 us
  Pallas kernels  38.3 us (82%)
  local copies, waits for them, and re-layouts  5.14 us (11%)
  other arithmetic  2.13 us (5%)
  between operations  0.7 us (1%)
    pallas_call x1, Pallas kernels, local(): pl.pallas_call(functools.partial(step_kernel, n_rep, n_ten, kvh_all, kvh)...  38.3 us
    unnamed x4, local copies, waits for them, and re-layouts  2.96 us

profile of v3, /device:TPU:8, one launch (start us, length us, event | category | flops | bytes accessed | tf_op | source)
XLA Modules:
  0.0 46.4 jit_solution(13168052268722534593)
XLA Ops:
  0.6 0.0 copy-start
  0.7 0.7 %multiply_add_fusion = s32[1024]{0:T(1024)S(1)} fusion(s32[1024]{0:T(1024)} %param.12, s32[1024]{0:T(1024)} %param.11), kind=kLoop, calls=%fused_computation.22 | loop fusion | flops 2048 | bytes 12288 | tf_op jit(solution)/shard_map/add | solution.py:259
  1.4 0.1 reshape.145
  1.5 0.2 convert_reduce_fusion
  1.7 0.1 convolution_convert_fusion
  1.8 0.4 select_reduce_fusion
  2.2 0.1 iota_add_fusion
  2.3 0.7 %add.93.slot_ref = s32[1,256]{1,0:T(1,128)} reshape(s32[64,4]{1,0:T(8,128)S(1)} %iota_add_fusion) | data formatting | bytes 2048 | tf_op jit(solution)/shard_map/add | solution.py:266
  3.0 0.1 broadcast_in_dim.14
  3.0 0.7 %reshape.146.code_ref = s32[1,512]{1,0:T(1,128)} reshape(s32[16,8,4]{2,1,0:T(8,128)S(1)} %broadcast_in_dim.14) | data formatting | bytes 4096 | tf_op jit(solution)/shard_map/reshape | solution.py:277
  3.7 0.7 %fusion.perm_ref = bf16[256,256]{1,0:T(8,128)(2,1)} fusion(s32[256]{0:T(256)S(1)} %fusion.9), kind=kLoop, calls=%fused_computation.2 | loop fusion | flops 131072 | bytes 132096 | tf_op jit(solution)/shard_map/convert_element_type | solution.py:284
  4.5 0.0 copy-done
  4.5 0.7 %broadcast_bitcast_fusion.fresh_ref = bf16[8,32,256]{2,1,0:T(8,128)(2,1)} fusion(bf16[8,4,256]{2,1,0:T(4,128)(2,1)S(1)} %copy-done), kind=kLoop, calls=%fused_computation.3 | loop fusion | bytes 147456 | tf_op jit(solution)/shard_map/reshape | solution.py:287
  5.1 38.3 %shard_map.104 = (bf16[8,32,128]{2,1,0:T(8,128)(2,1)}, bf16[8,32,128]{2,1,0:T(8,128)(2,1)}) custom-call(s32[8]{0:T(128)} %len_ref.1, s32[1,256]{1,0:T(1,128)} %add.93.slot_ref, s32[1,512]{1,0:T(1,128)} %reshape.146.code_ref, bf16[256,256]{1,0:T(8,128)(2,1)} %fusion.perm_ref, bf16[64,4,3840]{2,1,0:T(4,128)(2,1)} %feat_ref.1, bf16[30720,256]{1,0:T(8,128)(2,1)} %bitcast.16, ...), custom_call_target="tpu_custom_call" | custom-call | tf_op jit(solution)/shard_map/pallas_call | solution.py:295
  43.4 1.5 %copy.13 = bf16[8,32,128]{2,1,0:T(8,128)(2,1)} copy(bf16[8,32,128]{2,1,0:T(8,128)(2,1)} %get-tuple-element.4) | data formatting | bytes 131072
  44.9 1.5 %copy.14 = bf16[8,32,128]{2,1,0:T(8,128)(2,1)} copy(bf16[8,32,128]{2,1,0:T(8,128)(2,1)} %get-tuple-element.5) | data formatting | bytes 131072
  (7 shorter events, 0.1 us)
Async XLA Ops:
  0.6 3.8 %copy-start = (bf16[8,4,256]{2,1,0:T(4,128)(2,1)S(1)}, bf16[8,4,256]{2,1,0:T(4,128)(2,1)}, u32[]{:S(2)}) copy-start(bf16[8,4,256]{2,1,0:T(4,128)(2,1)} %param.16) | copy-start | bytes 49156

commit v4 on v3

--- a/solution.py
+++ b/solution.py
@@ -18,18 +18,26 @@
     n_ten,
     kvh_all,
     kvh,
+    slot_cap,
+    ids_ref,
+    len_hbm,
+    feat_hbm,
+    w_ref,
+    cq_hbm,
+    sq_hbm,
+    cache_hbm,
+    fresh_hbm,
+    cross_ref,
+    self_ref,
     len_ref,
+    feat_ref,
+    cq_ref,
+    sq_ref,
+    cache_ref,
+    fresh_ref,
     slot_ref,
     code_ref,
     perm_ref,
-    feat_ref,
-    w_ref,
-    cq_ref,
-    sq_ref,
-    cache_hbm,
-    fresh_ref,
-    cross_ref,
-    self_ref,
     feat,
     by_head,
     acc,
@@ -38,8 +46,8 @@
     outgoing,
     arrived,
     weights,
-    cache_ref,
-    cache_sem,
+    feat_sem,
+    in_sem,
     send_t,
     recv_t,
     send_r,
@@ -58,7 +66,26 @@
     rows, chunk = feat.shape[1:]
     run = 256 // kvh_all
     tile = run * kvh_all
-    cache_copy = pltpu.make_async_copy(cache_hbm, cache_ref, cache_sem)
+    patches = slot_rows // slot_cap
+    later = [
+        pltpu.make_async_copy(source, target, in_sem.at[i])
+        for i, (source, target) in enumerate(
+            (
+                (len_hbm, len_ref),
+                (cq_hbm, cq_ref),
+                (sq_hbm, sq_ref),
+                (cache_hbm, cache_ref),
+                (fresh_hbm, fresh_ref),
+            )
+        )
+    ]
+
+    def feat_copy(k):
+        if feat_ref.shape[0] == 1:
+            source = feat_hbm
+        else:
+            source = feat_hbm.at[:, :, pl.ds(pl.multiple_of(k * chunk, 128), chunk)]
+        return pltpu.make_async_copy(source, feat_ref.at[k], feat_sem.at[k])
 
     def to_ten(which, d):
         peer = lax.rem(ten + d, n_ten)
@@ -115,11 +142,60 @@
         for d in range(1, n_rep):
             peer = lax.rem(rep + d, n_rep)
             pl.semaphore_signal(barrier, inc=1, device_id=(peer, ten), device_id_type=MESH)
-        cache_copy.start()
+        for k in range(feat_ref.shape[0]):
+            feat_copy(k).start()
+        for copy in later:
+            copy.start()
+        at = lax.broadcasted_iota(jnp.int32, (tile, tile), 0)
+        lane = lax.broadcasted_iota(jnp.int32, (tile, tile), 1)
+        perm_ref[...] = (lane == lax.rem(at, run) * kvh_all + at // run).astype(BF16)
+
+        ids = ids_ref[...]
+        images = ids.shape[1]
+        at = lax.broadcasted_iota(jnp.int32, (images, images), 0)
+        lane = lax.broadcasted_iota(jnp.int32, (images, images), 1)
+        mine = (ids_ref[pl.ds(rep, 1), :] // reqs).astype(F32)
+        mine_col = jnp.sum(jnp.where(at == lane, mine, 0.0), axis=1, keepdims=True)
+        earlier = (mine_col == mine) & (lane < at)
+        rank = jnp.sum(jnp.where(earlier, 1.0, 0.0), axis=1, keepdims=True)
+        slot = (mine_col * slot_cap + rank) * patches
+        at_row = lax.broadcasted_iota(jnp.int32, (images, rows), 0)
+        lane_row = lax.broadcasted_iota(jnp.int32, (images, rows), 1)
+        slot = jnp.where(
+            at_row == lane_row // patches, slot + lax.rem(lane_row, patches).astype(F32), 0.0
+        )
+        slot_ref[...] = jnp.sum(slot, axis=0, keepdims=True).astype(jnp.int32)
+
+        match = ids // reqs == rep
+        before = (at < lane).astype(BF16)
+        place = jnp.dot(
+            jnp.where(match, 1.0, 0.0).astype(BF16), before, preferred_element_type=F32
+        )
+        size = n_rep * slot_rows
+        pick = (
+            lax.broadcasted_iota(jnp.int32, (size, n_rep), 1)
+            == lax.broadcasted_iota(jnp.int32, (size, n_rep), 0) // slot_rows
+        ).astype(BF16)
+        placed = jnp.dot(
+            pick, jnp.where(match, place + 1.0, 0.0).astype(BF16), preferred_element_type=F32
+        )
+        asked = jnp.where(match, (lax.rem(ids, reqs) + 1).astype(F32), 0.0)
+        asked = jnp.dot(pick, asked.astype(BF16), preferred_element_type=F32)
+        at = lax.broadcasted_iota(jnp.int32, (size, images), 0)
+        want = (lax.rem(at, slot_rows) // patches + 1).astype(F32)
+        code = jnp.sum(jnp.where(placed == want, asked, 0.0), axis=1, keepdims=True) - 1.0
+        for first in range(0, size, 128):
+            at = lax.broadcasted_iota(jnp.int32, (128, 128), 0)
+            lane = lax.broadcasted_iota(jnp.int32, (128, 128), 1)
+            turned = jnp.where(at == lane, code[first : first + 128], 0.0)
+            code_ref[:, first : first + 128] = jnp.sum(turned, axis=0, keepdims=True).astype(
+                jnp.int32
+            )
 
     @pl.when(half == 0)
     def _():
-        feat[step] = feat_ref[...].astype(F32).reshape(rows, chunk).astype(BF16)
+        feat_copy(step).wait()
+        feat[step] = feat_ref[step].astype(F32).reshape(rows, chunk).astype(BF16)
 
     @pl.when(step == 0)
     def _():
@@ -165,7 +241,8 @@
             to_ten(1, d).start()
         route(1)
 
-        cache_copy.wait()
+        for copy in later:
+            copy.wait()
         places = cache_ref.shape[1] * kvh
         col = lax.broadcasted_iota(jnp.int32, (heads, places), 1)
         row = lax.broadcasted_iota(jnp.int32, (heads, places), 0)
@@ -181,7 +258,9 @@
             )
             live = same_head & (col // kvh < len_ref[b])
             weight = jnp.where(live, jnp.exp(score), 0.0)
-            fresh = fresh_ref[b].astype(F32)
+            fresh = jnp.broadcast_to(
+                fresh_ref[b].astype(F32)[:, None, :], (kvh, group, 2 * width)
+            ).reshape(heads, 2 * width)
             fresh_weight = jnp.exp(
                 jnp.sum(query.astype(F32) * fresh[:, :width], axis=1, keepdims=True) * scale
             )
@@ -246,7 +325,6 @@
     fresh_key_value,
     cache_len,
 ):
-    me = lax.axis_index("replica")
     images, patches, depth = features.shape
     reqs, heads, width = cross_query.shape
     kvh = self_cache.shape[2]
@@ -257,57 +335,27 @@
     slot_rows = slot_cap * patches
 
     ids = (image_owner * reqs + image_request).reshape(n_rep, images)
-    owners = ids // reqs
-    mine = lax.dynamic_index_in_dim(ids, me, 0, keepdims=False) // reqs
-    at = jnp.arange(images, dtype=jnp.int32)
-    earlier = (mine[:, None] == mine[None, :]) & (at[:, None] > at[None, :])
-    rank = jnp.sum(earlier.astype(jnp.int32), axis=1, dtype=jnp.int32)
-    slot = mine * slot_cap + rank
-    slot_row = (slot[:, None] * patches + jnp.arange(patches, dtype=jnp.int32)[None, :]).reshape(
-        1, rows
-    )
-
-    match = owners == me
-    before = (at[:, None] < at[None, :]).astype(BF16)
-    place = jnp.dot(match.astype(BF16), before, preferred_element_type=F32).astype(jnp.int32)
-    chosen = match[:, None, :] & (
-        place[:, None, :] == jnp.arange(slot_cap, dtype=jnp.int32)[None, :, None]
-    )
-    code = jnp.sum(jnp.where(chosen, (ids - me * reqs)[:, None, :] + 1, 0), axis=-1) - 1
-    code = jnp.broadcast_to(code[:, :, None], (n_rep, slot_cap, patches)).reshape(
-        1, n_rep * slot_rows
-    )
-
-    tile = 256 // kvh_all * kvh_all
-    spot = jnp.arange(tile, dtype=jnp.int32)
-    origin = (spot % (tile // kvh_all)) * kvh_all + spot // (tile // kvh_all)
-    perm = (origin[:, None] == spot[None, :]).astype(BF16)
-    fresh = jnp.broadcast_to(
-        fresh_key_value[:, :, None, :], (reqs, kvh, group, 2 * width)
-    ).reshape(reqs, heads, 2 * width)
     chunk = depth
     for c in range(256, 769, 256):
         if depth % c == 0:
             chunk = c
     steps = depth // chunk
     cols = kvh * width
+    tile = 256 // kvh_all * kvh_all
     vmem = pl.BlockSpec(memory_space=pltpu.VMEM)
+    hbm = pl.BlockSpec(memory_space=pltpu.HBM)
     return pl.pallas_call(
-        functools.partial(step_kernel, n_rep, n_ten, kvh_all, kvh),
+        functools.partial(step_kernel, n_rep, n_ten, kvh_all, kvh, slot_cap),
         grid=(2, steps),
         in_specs=[
-            pl.BlockSpec(memory_space=pltpu.SMEM),
             vmem,
-            vmem,
-            vmem,
-            pl.BlockSpec(
-                (images, patches, chunk), lambda j, k: (0, 0, k * (1 - j) + (steps - 1) * j)
-            ),
+            hbm,
+            hbm,
             pl.BlockSpec((chunk * kvh_all, width), lambda j, k: (k, j)),
-            vmem,
-            vmem,
-            pl.BlockSpec(memory_space=pl.ANY),
-            vmem,
+            hbm,
+            hbm,
+            hbm,
+            hbm,
         ],
         out_specs=(vmem, vmem),
         out_shape=(
@@ -315,6 +363,15 @@
             jax.ShapeDtypeStruct(self_query.shape, BF16),
         ),
         scratch_shapes=[
+            pltpu.SMEM(cache_len.shape, jnp.int32),
+            pltpu.VMEM((steps, images, patches, chunk), BF16),
+            pltpu.VMEM(cross_query.shape, BF16),
+            pltpu.VMEM(self_query.shape, BF16),
+            pltpu.VMEM(self_cache.shape, BF16),
+            pltpu.VMEM(fresh_key_value.shape, BF16),
+            pltpu.VMEM((1, rows), jnp.int32),
+            pltpu.VMEM((1, n_rep * slot_rows), jnp.int32),
+            pltpu.VMEM((tile, tile), BF16),
             pltpu.VMEM((steps, rows, chunk), BF16),
             pltpu.VMEM((kvh_all // 2, chunk, 2 * width), BF16),
             pltpu.VMEM((rows, kvh_all * width), F32),
@@ -323,8 +380,8 @@
             pltpu.VMEM((2, n_rep, slot_rows, cols), BF16),
             pltpu.VMEM((2, n_rep, slot_rows, cols), BF16),
             pltpu.VMEM((kvh, reqs * group, n_rep * slot_rows), BF16),
-            pltpu.VMEM(self_cache.shape, BF16),
-            pltpu.SemaphoreType.DMA,
+            pltpu.SemaphoreType.DMA((steps,)),
+            pltpu.SemaphoreType.DMA((5,)),
             pltpu.SemaphoreType.DMA((2, n_ten - 1)),
             pltpu.SemaphoreType.DMA((2, n_ten - 1)),
             pltpu.SemaphoreType.DMA((2, n_rep)),
@@ -336,16 +393,14 @@
             vmem_limit_bytes=60 * 1024 * 1024,
         ),
     )(
+        ids,
         cache_len,
-        slot_row,
-        code,
-        perm,
         features,
         kv_weight.reshape(depth * kvh_all, 2 * width),
         cross_query,
         self_query,
         self_cache,
-        fresh,
+        fresh_key_value,
     )
 
 

time: 46.7 us -> 44 us (0.942)
  local copies, waits for them, and re-layouts: 5.14 us -> 3.61 us
  other arithmetic: 2.13 us -> 0.71 us
    reshape x2 -> x0, local copies, waits for them, and re-layouts: 1.36 us -> none  [the longest x1 0.7 us: local(): jnp.broadcast_to(code[:, :, None], (n_rep, slot_cap, patches))]
    convert_element_type x1 -> x0, other arithmetic: 0.74 us -> none  [local(): perm = (origin[:, None] == spot[None, :]).astype(BF16)]
    add x1 -> x0, local copies, waits for them, and re-layouts: 0.68 us -> none  [local(): slot[:, None] * patches + jnp.arange(patches, dtype=jnp.int32)[None, :]]
    reshape x1, local copies, waits for them, and re-layouts: 0.07 us -> 0.67 us  [local(): ids = (image_owner * reqs + image_request).reshape(n_rep, images)]
    reduce_sum x2 -> x0, other arithmetic: 0.53 us -> none  [the longest x1 0.35 us: local(): jnp.sum(jnp.where(chosen, (ids - me * reqs)[:, None, :] + 1, 0), axis=-1)]
    unnamed x4 -> x2, local copies, waits for them, and re-layouts: 2.96 us -> 2.95 us
where the time goes in v4:
time: 44 us; the launch traced here: 43.6 us
  Pallas kernels  38.6 us (88%)
  local copies, waits for them, and re-layouts  3.61 us (8%)
  other arithmetic  0.71 us (2%)
  between operations  0.64 us (1%)
    pallas_call x1, Pallas kernels, local(): pl.pallas_call(functools.partial(step_kernel, n_rep, n_ten, kvh_all, kvh,...  38.6 us
    unnamed x2, local copies, waits for them, and re-layouts  2.95 us

profile of v4, /device:TPU:8, one launch (start us, length us, event | category | flops | bytes accessed | tf_op | source)
XLA Modules:
  0.0 43.6 jit_solution(5945211399565371058)
XLA Ops:
  0.6 0.7 %multiply_add_fusion = s32[1024]{0:T(1024)S(1)} fusion(s32[1024]{0:T(1024)} %param.12, s32[1024]{0:T(1024)} %param.11), kind=kLoop, calls=%fused_computation | loop fusion | flops 2048 | bytes 12288 | tf_op jit(solution)/shard_map/add | solution.py:337
  1.3 0.7 %reshape.10.ids_ref = s32[16,64]{1,0:T(8,128)} reshape(s32[1024]{0:T(1024)S(1)} %multiply_add_fusion) | data formatting | bytes 8192 | tf_op jit(solution)/shard_map/reshape | solution.py:337
  2.0 38.6 %shard_map.104 = (bf16[8,32,128]{2,1,0:T(8,128)(2,1)}, bf16[8,32,128]{2,1,0:T(8,128)(2,1)}) custom-call(s32[16,64]{1,0:T(8,128)} %reshape.10.ids_ref, s32[8]{0:T(128)} %len_hbm.1, bf16[64,4,3840]{2,1,0:T(4,128)(2,1)} %feat_hbm.1, bf16[30720,256]{1,0:T(8,128)(2,1)} %bitcast.1, bf16[8,32,128]{2,1,0:T(8,128)(2,1)} %cq_hbm.1, bf16[8,32,128]{2,1,0:T(8,128)(2,1)} %sq_hbm.1, ...), custom_call_target="tpu_custom_call" | custom-call | tf_op jit(solution)/shard_map/pallas_call | solution.py:347
  40.7 1.5 %copy.13 = bf16[8,32,128]{2,1,0:T(8,128)(2,1)} copy(bf16[8,32,128]{2,1,0:T(8,128)(2,1)} %get-tuple-element.4) | data formatting | bytes 131072
  42.1 1.5 %copy.14 = bf16[8,32,128]{2,1,0:T(8,128)(2,1)} copy(bf16[8,32,128]{2,1,0:T(8,128)(2,1)} %get-tuple-element.5) | data formatting | bytes 131072

commit v5 on v4

--- a/solution.py
+++ b/solution.py
@@ -19,7 +19,8 @@
     kvh_all,
     kvh,
     slot_cap,
-    ids_ref,
+    owner_ref,
+    request_ref,
     len_hbm,
     feat_hbm,
     w_ref,
@@ -35,6 +36,7 @@
     sq_ref,
     cache_ref,
     fresh_ref,
+    ids_ref,
     slot_ref,
     code_ref,
     perm_ref,
@@ -129,7 +131,7 @@
             kv = kv + got[which, d - 1].astype(F32)
         placed = jnp.dot(placing, kv.astype(BF16), preferred_element_type=F32)
         outgoing[which] = placed.reshape(n_rep, slot_rows, cols).astype(BF16)
-        for d in range(1, n_rep):
+        for d in sorted(range(1, n_rep), key=lambda d: abs(d - n_rep // 2)):
             to_rep(which, d).start()
         arrived[which, rep] = outgoing[which, rep]
 
@@ -150,8 +152,15 @@
         lane = lax.broadcasted_iota(jnp.int32, (tile, tile), 1)
         perm_ref[...] = (lane == lax.rem(at, run) * kvh_all + at // run).astype(BF16)
 
+        images = ids_ref.shape[1]
+        lanes = owner_ref.shape[1]
+        for b in range(n_rep):
+            r, c = divmod(b * images, lanes)
+            ids_ref[b : b + 1, :] = (
+                owner_ref[r : r + 1, c : c + images] * reqs
+                + request_ref[r : r + 1, c : c + images]
+            )
         ids = ids_ref[...]
-        images = ids.shape[1]
         at = lax.broadcasted_iota(jnp.int32, (images, images), 0)
         lane = lax.broadcasted_iota(jnp.int32, (images, images), 1)
         mine = (ids_ref[pl.ds(rep, 1), :] // reqs).astype(F32)
@@ -231,7 +240,7 @@
         for d in range(1, n_ten):
             to_ten(0, d).start()
 
-    @pl.when((half == 1) & (step == jnp.minimum(1, steps - 1)))
+    @pl.when((half == 1) & (step == 0))
     def _():
         route(0)
 
@@ -310,6 +319,15 @@
                 to_ten(which, d).wait_send()
             for d in range(1, n_rep):
                 to_rep(which, d).wait_send()
+
+
+def hand_out_kernel(cross_in, self_in, cross_out, self_out, sems):
+    first = pltpu.make_async_copy(cross_in, cross_out, sems.at[0])
+    second = pltpu.make_async_copy(self_in, self_out, sems.at[1])
+    first.start()
+    second.start()
+    first.wait()
+    second.wait()
 
 
 def local(
@@ -334,7 +352,7 @@
     rows = images * patches
     slot_rows = slot_cap * patches
 
-    ids = (image_owner * reqs + image_request).reshape(n_rep, images)
+    lanes = 128 // math.gcd(128, images) * images
     chunk = depth
     for c in range(256, 769, 256):
         if depth % c == 0:
@@ -344,10 +362,11 @@
     tile = 256 // kvh_all * kvh_all
     vmem = pl.BlockSpec(memory_space=pltpu.VMEM)
     hbm = pl.BlockSpec(memory_space=pltpu.HBM)
-    return pl.pallas_call(
+    cross, own = pl.pallas_call(
         functools.partial(step_kernel, n_rep, n_ten, kvh_all, kvh, slot_cap),
         grid=(2, steps),
         in_specs=[
+            vmem,
             vmem,
             hbm,
             hbm,
@@ -369,6 +388,7 @@
             pltpu.VMEM(self_query.shape, BF16),
             pltpu.VMEM(self_cache.shape, BF16),
             pltpu.VMEM(fresh_key_value.shape, BF16),
+            pltpu.VMEM((n_rep, images), jnp.int32),
             pltpu.VMEM((1, rows), jnp.int32),
             pltpu.VMEM((1, n_rep * slot_rows), jnp.int32),
             pltpu.VMEM((tile, tile), BF16),
@@ -393,7 +413,8 @@
             vmem_limit_bytes=60 * 1024 * 1024,
         ),
     )(
-        ids,
+        image_owner.reshape(n_rep * images // lanes, lanes),
+        image_request.reshape(n_rep * images // lanes, lanes),
         cache_len,
         features,
         kv_weight.reshape(depth * kvh_all, 2 * width),
@@ -402,6 +423,18 @@
         self_cache,
         fresh_key_value,
     )
+    anywhere = pl.BlockSpec(memory_space=pl.ANY)
+    return pl.pallas_call(
+        hand_out_kernel,
+        in_specs=[anywhere, anywhere],
+        out_specs=(anywhere, anywhere),
+        out_shape=(
+            jax.ShapeDtypeStruct(cross.shape, BF16),
+            jax.ShapeDtypeStruct(own.shape, BF16),
+        ),
+        scratch_shapes=[pltpu.SemaphoreType.DMA((2,))],
+        compiler_params=pltpu.CompilerParams(vmem_limit_bytes=60 * 1024 * 1024),
+    )(cross, own)
 
 
 def solution(mesh):

time: 44 us -> 46.5 us (1.057)
  the two profiles are of different devices: /device:TPU:8 before, /device:TPU:0 now
where the time goes in v5:
time: 46.5 us; the launch traced here: 46.2 us
  Pallas kernels  45.6 us (98%)
  between operations  0.64 us (1%)
    pallas_call x1, Pallas kernels, local(): pl.pallas_call(functools.partial(step_kernel, n_rep, n_ten, kvh_all, kvh,...  40.5 us
    pallas_call x1, Pallas kernels, local(): pl.pallas_call(hand_out_kernel, in_specs=[anywhere, anywhere], out_specs=...  5.09 us

profile of v5, /device:TPU:0, one launch (start us, length us, event | category | flops | bytes accessed | tf_op | source)
XLA Modules:
  0.0 46.2 jit_solution(18284291544449826036)
XLA Ops:
  0.6 40.5 %shard_map.104 = (bf16[8,32,128]{2,1,0:T(8,128)(2,1)}, bf16[8,32,128]{2,1,0:T(8,128)(2,1)}) custom-call(s32[8,128]{1,0:T(8,128)} %bitcast.4, s32[8,128]{1,0:T(8,128)} %bitcast.5, s32[8]{0:T(128)} %len_hbm.1, bf16[64,4,3840]{2,1,0:T(4,128)(2,1)} %feat_hbm.1, bf16[30720,256]{1,0:T(8,128)(2,1)} %bitcast.3, bf16[8,32,128]{2,1,0:T(8,128)(2,1)} %cq_hbm.1, ...), custom_call_target="tpu_custom_call" | custom-call | tf_op jit(solution)/shard_map/pallas_call | solution.py:365
  41.1 5.1 %shard_map.105 = (bf16[8,32,128]{2,1,0:T(8,128)(2,1)}, bf16[8,32,128]{2,1,0:T(8,128)(2,1)}) custom-call(bf16[8,32,128]{2,1,0:T(8,128)(2,1)} %get-tuple-element.4.cross_in, bf16[8,32,128]{2,1,0:T(8,128)(2,1)} %get-tuple-element.5.self_in), custom_call_target="tpu_custom_call" | custom-call | tf_op jit(solution)/shard_map/pallas_call | solution.py:427

commit v6 on v4

--- a/solution.py
+++ b/solution.py
@@ -19,7 +19,8 @@
     kvh_all,
     kvh,
     slot_cap,
-    ids_ref,
+    owner_ref,
+    request_ref,
     len_hbm,
     feat_hbm,
     w_ref,
@@ -35,6 +36,7 @@
     sq_ref,
     cache_ref,
     fresh_ref,
+    ids_ref,
     slot_ref,
     code_ref,
     perm_ref,
@@ -150,8 +152,15 @@
         lane = lax.broadcasted_iota(jnp.int32, (tile, tile), 1)
         perm_ref[...] = (lane == lax.rem(at, run) * kvh_all + at // run).astype(BF16)
 
+        images = ids_ref.shape[1]
+        lanes = owner_ref.shape[1]
+        for b in range(n_rep):
+            r, c = divmod(b * images, lanes)
+            ids_ref[b : b + 1, :] = (
+                owner_ref[r : r + 1, c : c + images] * reqs
+                + request_ref[r : r + 1, c : c + images]
+            )
         ids = ids_ref[...]
-        images = ids.shape[1]
         at = lax.broadcasted_iota(jnp.int32, (images, images), 0)
         lane = lax.broadcasted_iota(jnp.int32, (images, images), 1)
         mine = (ids_ref[pl.ds(rep, 1), :] // reqs).astype(F32)
@@ -231,7 +240,7 @@
         for d in range(1, n_ten):
             to_ten(0, d).start()
 
-    @pl.when((half == 1) & (step == jnp.minimum(1, steps - 1)))
+    @pl.when((half == 1) & (step == 0))
     def _():
         route(0)
 
@@ -334,7 +343,7 @@
     rows = images * patches
     slot_rows = slot_cap * patches
 
-    ids = (image_owner * reqs + image_request).reshape(n_rep, images)
+    lanes = 128 // math.gcd(128, images) * images
     chunk = depth
     for c in range(256, 769, 256):
         if depth % c == 0:
@@ -349,6 +358,7 @@
         grid=(2, steps),
         in_specs=[
             vmem,
+            vmem,
             hbm,
             hbm,
             pl.BlockSpec((chunk * kvh_all, width), lambda j, k: (k, j)),
@@ -369,6 +379,7 @@
             pltpu.VMEM(self_query.shape, BF16),
             pltpu.VMEM(self_cache.shape, BF16),
             pltpu.VMEM(fresh_key_value.shape, BF16),
+            pltpu.VMEM((n_rep, images), jnp.int32),
             pltpu.VMEM((1, rows), jnp.int32),
             pltpu.VMEM((1, n_rep * slot_rows), jnp.int32),
             pltpu.VMEM((tile, tile), BF16),
@@ -393,7 +404,8 @@
             vmem_limit_bytes=60 * 1024 * 1024,
         ),
     )(
-        ids,
+        image_owner.reshape(n_rep * images // lanes, lanes),
+        image_request.reshape(n_rep * images // lanes, lanes),
         cache_len,
         features,
         kv_weight.reshape(depth * kvh_all, 2 * width),

time: 44 us -> 41.8 us (0.950)
  Pallas kernels: 38.6 us -> 37.4 us
  other arithmetic: 0.71 us -> 0 us
  local copies, waits for them, and re-layouts: 3.61 us -> 2.95 us
    pallas_call x1, Pallas kernels: 38.6 us -> 37.4 us  [local(): pl.pallas_call(functools.partial(step_kernel, n_rep, n_ten, kvh_all, kvh,...]
    add x1 -> x0, other arithmetic: 0.71 us -> none  [local(): ids = (image_owner * reqs + image_request).reshape(n_rep, images)]
    reshape x1 -> x0, local copies, waits for them, and re-layouts: 0.67 us -> none  [local(): ids = (image_owner * reqs + image_request).reshape(n_rep, images)]
where the time goes in v6:
time: 41.8 us; the launch traced here: 41 us
  Pallas kernels  37.4 us (89%)
  local copies, waits for them, and re-layouts  2.95 us (7%)
  between operations  0.64 us (2%)
    pallas_call x1, Pallas kernels, local(): pl.pallas_call(functools.partial(step_kernel, n_rep, n_ten, kvh_all, kvh,...  37.4 us
    unnamed x2, local copies, waits for them, and re-layouts  2.95 us

profile of v6, /device:TPU:8, one launch (start us, length us, event | category | flops | bytes accessed | tf_op | source)
XLA Modules:
  0.0 41.0 jit_solution(1967992966641664075)
XLA Ops:
  0.6 37.4 %shard_map.104 = (bf16[8,32,128]{2,1,0:T(8,128)(2,1)}, bf16[8,32,128]{2,1,0:T(8,128)(2,1)}) custom-call(s32[8,128]{1,0:T(8,128)} %bitcast.4, s32[8,128]{1,0:T(8,128)} %bitcast.5, s32[8]{0:T(128)} %len_hbm.1, bf16[64,4,3840]{2,1,0:T(4,128)(2,1)} %feat_hbm.1, bf16[30720,256]{1,0:T(8,128)(2,1)} %bitcast.3, bf16[8,32,128]{2,1,0:T(8,128)(2,1)} %cq_hbm.1, ...), custom_call_target="tpu_custom_call" | custom-call | tf_op jit(solution)/shard_map/pallas_call | solution.py:356
  38.0 1.5 %copy.13 = bf16[8,32,128]{2,1,0:T(8,128)(2,1)} copy(bf16[8,32,128]{2,1,0:T(8,128)(2,1)} %get-tuple-element.4) | data formatting | bytes 131072
  39.5 1.5 %copy.14 = bf16[8,32,128]{2,1,0:T(8,128)(2,1)} copy(bf16[8,32,128]{2,1,0:T(8,128)(2,1)} %get-tuple-element.5) | data formatting | bytes 131072
